TPU v7x, 32 devices: a whole 2x2x4 slice. The times are simulated.
32 devices in a mesh: dp: 8 (over y, x, core), seq: 4 (over z).
Axes of the slice: x: 2, y: 2, z: 4, core: 2. Of those that a mesh axis runs over, the one named last changes fastest.
Arguments:
- queries: bfloat16 [8, 512, 2048], P('dp', 'seq'), may hold values from -5 to 5
- keys: bfloat16 [8, 512, 512], P('dp', 'seq'), may hold values from -5 to 5
- values: bfloat16 [8, 512, 512], P('dp', 'seq'), may hold values from -6 to 6
- upstream: bfloat16 [8, 512, 2048], P('dp', 'seq'), may hold values from -6 to 6
- doc_ids: int32 [8, 512], P('dp', 'seq'), may hold values from 0 to 11, never falling along the last dimension, each value on 1 to 64 neighbouring positions
Outputs:
- attended: bfloat16 [8, 512, 2048], P('dp', 'seq')
- query_grad: bfloat16 [8, 512, 2048], P('dp', 'seq')
- key_gradient: bfloat16 [8, 512, 512], P('dp', 'seq')
- value_gradient: bfloat16 [8, 512, 512], P('dp', 'seq')
Inputs may be any that keep to these rules, and one draw needn't show every extreme that they name: `doc_ids`: in every row the document number never falls along the positions; each document holds at most 64 positions, and one holds exactly 64.
All inputs are finite; a program needn't handle non-finite values.
Results may differ from a plain program's by a relative error of at most 0.018.
Values may be sent and summed in bfloat16 or wider, within the bound.
A program may use at most 64 MiB of HBM per device.

v0:
```python
import math

import jax
import jax.numpy as jnp
from jax import lax
from jax.sharding import PartitionSpec as P

QUERY_HEADS = 16
KEY_VALUE_HEADS = 4
HEAD_DIMENSION = 128


def attend(queries, keys, values, upstream, doc_row):
    seq_rows = queries.shape[0]
    scaling = 1.0 / math.sqrt(queries.shape[2])
    block_rows = min(512, seq_rows)
    longest = seq_rows // 8
    positions = lax.iota(jnp.int32, seq_rows)
    key_gradient = jnp.zeros(keys.shape, jnp.float32)
    value_gradient = jnp.zeros(values.shape, jnp.float32)
    attended_parts = []
    query_parts = []
    for number in range(seq_rows // block_rows):
        start_row = number * block_rows
        finish = start_row + block_rows
        lowest = max(0, start_row - longest)
        query_block = queries[start_row:finish]
        upstream_block = upstream[start_row:finish]
        key_part = keys[lowest:finish]
        value_part = values[lowest:finish]
        scores = (
            jnp.einsum("qhd,khd->hqk", query_block, key_part, preferred_element_type=jnp.float32)
            * scaling
        )
        allowed = (doc_row[None, lowest:finish] == doc_row[start_row:finish, None]) & (
            positions[None, lowest:finish] <= positions[start_row:finish, None]
        )
        scores = jnp.where(allowed[None], scores, -jnp.inf)
        largest = jnp.max(scores, axis=2, keepdims=True)
        weights = jnp.exp(scores - largest)
        normalized = weights / jnp.sum(weights, axis=2, keepdims=True)
        probs_half = normalized.astype(jnp.bfloat16)
        attended_block = jnp.einsum(
            "hqk,khd->qhd", probs_half, value_part, preferred_element_type=jnp.float32
        ).astype(jnp.bfloat16)
        row_delta = jnp.sum(
            upstream_block.astype(jnp.float32) * attended_block.astype(jnp.float32), axis=2
        ).T[:, :, None]
        prob_grad = jnp.einsum(
            "qhd,khd->hqk", upstream_block, value_part, preferred_element_type=jnp.float32
        )
        score_grad = (normalized * (prob_grad - row_delta)).astype(jnp.bfloat16)
        query_parts.append(
            (
                jnp.einsum("hqk,khd->qhd", score_grad, key_part, preferred_element_type=jnp.float32)
                * scaling
            ).astype(jnp.bfloat16)
        )
        key_gradient = key_gradient.at[lowest:finish].add(
            jnp.einsum("hqk,qhd->khd", score_grad, query_block, preferred_element_type=jnp.float32)
            * scaling
        )
        value_gradient = value_gradient.at[lowest:finish].add(
            jnp.einsum(
                "hqk,qhd->khd", probs_half, upstream_block, preferred_element_type=jnp.float32
            )
        )
        attended_parts.append(attended_block)
    return (
        jnp.concatenate(attended_parts),
        jnp.concatenate(query_parts),
        key_gradient,
        value_gradient,
    )


def shards(queries, keys, values, upstream, doc_ids):
    tokens_per_shard = queries.shape[1]
    group_count = lax.axis_size("dp")
    packed_slab_rows = tokens_per_shard // group_count
    head_local = QUERY_HEADS // lax.axis_size("seq")
    queries_per_group = QUERY_HEADS // KEY_VALUE_HEADS
    query_rows, key_row_array, value_row_array, upstream_rows = (
        lax.all_to_all(
            queries.reshape(group_count, packed_slab_rows, QUERY_HEADS * HEAD_DIMENSION),
            "dp",
            split_axis=0,
            concat_axis=0,
            tiled=True,
        ),
        lax.all_to_all(
            keys.reshape(group_count, packed_slab_rows, KEY_VALUE_HEADS * HEAD_DIMENSION),
            "dp",
            split_axis=0,
            concat_axis=0,
            tiled=True,
        ),
        lax.all_to_all(
            values.reshape(group_count, packed_slab_rows, KEY_VALUE_HEADS * HEAD_DIMENSION),
            "dp",
            split_axis=0,
            concat_axis=0,
            tiled=True,
        ),
        lax.all_to_all(
            upstream.reshape(group_count, packed_slab_rows, QUERY_HEADS * HEAD_DIMENSION),
            "dp",
            split_axis=0,
            concat_axis=0,
            tiled=True,
        ),
    )
    query_tok = query_rows.reshape(tokens_per_shard, QUERY_HEADS, HEAD_DIMENSION)
    upstream_tok = upstream_rows.reshape(tokens_per_shard, QUERY_HEADS, HEAD_DIMENSION)
    key_tokens = key_row_array.reshape(tokens_per_shard, KEY_VALUE_HEADS, HEAD_DIMENSION)
    value_tokens = value_row_array.reshape(tokens_per_shard, KEY_VALUE_HEADS, HEAD_DIMENSION)
    doc_row = lax.all_gather(doc_ids, "seq", axis=1, tiled=True)[0]
    query_head_array, incoming_gradient_heads = (
        lax.all_to_all(query_tok, "seq", split_axis=1, concat_axis=0, tiled=True),
        lax.all_to_all(upstream_tok, "seq", split_axis=1, concat_axis=0, tiled=True),
    )
    key_whole, value_whole = (
        lax.all_gather(key_tokens, "seq", axis=0, tiled=True),
        lax.all_gather(value_tokens, "seq", axis=0, tiled=True),
    )
    head_ids = (
        lax.axis_index("seq") * head_local + lax.iota(jnp.int32, head_local)
    ) // queries_per_group
    key_head_array = jnp.take(key_whole, head_ids, axis=1)
    value_head_array = jnp.take(value_whole, head_ids, axis=1)
    attended, query_grad, key_gradient, value_gradient = attend(
        query_head_array, key_head_array, value_head_array, incoming_gradient_heads, doc_row
    )
    attended_back, query_back = (
        lax.all_to_all(attended, "seq", split_axis=0, concat_axis=1, tiled=True),
        lax.all_to_all(query_grad, "seq", split_axis=0, concat_axis=1, tiled=True),
    )
    key_backward, value_backward = (
        lax.all_to_all(key_gradient, "seq", split_axis=0, concat_axis=1, tiled=True),
        lax.all_to_all(value_gradient, "seq", split_axis=0, concat_axis=1, tiled=True),
    )
    key_gradient_total = jnp.sum(
        key_backward.reshape(tokens_per_shard, KEY_VALUE_HEADS, queries_per_group, HEAD_DIMENSION),
        axis=2,
    ).astype(jnp.bfloat16)
    value_gradient_total = jnp.sum(
        value_backward.reshape(
            tokens_per_shard, KEY_VALUE_HEADS, queries_per_group, HEAD_DIMENSION
        ),
        axis=2,
    ).astype(jnp.bfloat16)
    attended_out, query_out, key_result, value_result = (
        lax.all_to_all(
            attended_back.reshape(group_count, packed_slab_rows, QUERY_HEADS * HEAD_DIMENSION),
            "dp",
            split_axis=0,
            concat_axis=0,
            tiled=True,
        ),
        lax.all_to_all(
            query_back.reshape(group_count, packed_slab_rows, QUERY_HEADS * HEAD_DIMENSION),
            "dp",
            split_axis=0,
            concat_axis=0,
            tiled=True,
        ),
        lax.all_to_all(
            key_gradient_total.reshape(
                group_count, packed_slab_rows, KEY_VALUE_HEADS * HEAD_DIMENSION
            ),
            "dp",
            split_axis=0,
            concat_axis=0,
            tiled=True,
        ),
        lax.all_to_all(
            value_gradient_total.reshape(
                group_count, packed_slab_rows, KEY_VALUE_HEADS * HEAD_DIMENSION
            ),
            "dp",
            split_axis=0,
            concat_axis=0,
            tiled=True,
        ),
    )
    return (
        attended_out.reshape(1, tokens_per_shard, QUERY_HEADS * HEAD_DIMENSION),
        query_out.reshape(1, tokens_per_shard, QUERY_HEADS * HEAD_DIMENSION),
        key_result.reshape(1, tokens_per_shard, KEY_VALUE_HEADS * HEAD_DIMENSION),
        value_result.reshape(1, tokens_per_shard, KEY_VALUE_HEADS * HEAD_DIMENSION),
    )


def solution(mesh):
    in_specs = (
        P("dp", "seq", None),
        P("dp", "seq", None),
        P("dp", "seq", None),
        P("dp", "seq", None),
        P("dp", "seq"),
    )
    out_specs = (
        P("dp", "seq", None),
        P("dp", "seq", None),
        P("dp", "seq", None),
        P("dp", "seq", None),
    )
    return jax.shard_map(shards, mesh=mesh, in_specs=in_specs, out_specs=out_specs, check_vma=False)
```

profile of v0, /device:TPU:0, one launch (start us, length us, event | category | flops | bytes accessed | tf_op | source)
XLA Modules:
  0.0 268.6 jit_solution(4736134890844970672)
XLA Ops:
  0.6 10.7 %all_to_all.124 = bf16[8,16,512]{2,1,0:T(8,128)(2,1)S(1)} all-to-all(bf16[8,16,512]{2,1,0:T(8,128)(2,1)} %bitcast.98), channel_id=1, replica_groups=mesh['dp'=8,'seq'=4] {'dp'}, dimensions={0} | all-to-all | bytes 262144 | tf_op jit(solution)/shard_map/all_to_all | solution.py:91
  11.3 8.8 %all_to_all.125 = bf16[8,16,512]{2,1,0:T(8,128)(2,1)S(1)} all-to-all(bf16[8,16,512]{2,1,0:T(8,128)(2,1)} %bitcast.99), channel_id=1, replica_groups=mesh['dp'=8,'seq'=4] {'dp'}, dimensions={0} | all-to-all | bytes 262144 | tf_op jit(solution)/shard_map/all_to_all | solution.py:98
  20.1 13.3 %all_to_all.126 = bf16[8,16,2048]{2,1,0:T(8,128)(2,1)S(1)} all-to-all(bf16[8,16,2048]{2,1,0:T(8,128)(2,1)} %bitcast.94), channel_id=1, replica_groups=mesh['dp'=8,'seq'=4] {'dp'}, dimensions={0} | all-to-all | bytes 1048576 | tf_op jit(solution)/shard_map/all_to_all | solution.py:84
  33.4 3.5 %all-to-all-start.6 = ((bf16[8,16,2048]{2,1,0:T(8,128)(2,1)}), bf16[8,16,2048]{2,1,0:T(8,128)(2,1)S(1)}, u32[]{:S(2)}, u32[]{:S(2)}) async-start(bf16[8,16,2048]{2,1,0:T(8,128)(2,1)} %bitcast.95), calls=%async_computation.6 | async-start | bytes 1048576 | tf_op jit(solution)/shard_map/all_to_all | solution.py:105
  37.0 0.9 copy.43
  38.0 8.6 %all-to-all-done.6 = bf16[8,16,2048]{2,1,0:T(8,128)(2,1)S(1)} async-done(((bf16[8,16,2048]{2,1,0:T(8,128)(2,1)}), bf16[8,16,2048]{2,1,0:T(8,128)(2,1)S(1)}, u32[]{:S(2)}, u32[]{:S(2)}) %all-to-all-start.6) | async-done | bytes 524320 | tf_op jit(solution)/shard_map/all_to_all | solution.py:105
  46.6 4.9 %all-to-all-start.3 = ((bf16[128,16,128]{2,0,1:T(8,128)(2,1)}), bf16[128,16,128]{2,0,1:T(8,128)(2,1)S(1)}, u32[]{:S(2)}, u32[]{:S(2)}) async-start(bf16[128,16,128]{2,0,1:T(8,128)(2,1)} %copy.43), calls=%async_computation.3 | async-start | bytes 1048576 | tf_op jit(solution)/shard_map/all_to_all | solution.py:119
  51.6 0.9 copy.49
  52.5 11.1 %all-to-all-done.3 = bf16[128,16,128]{2,0,1:T(8,128)(2,1)S(1)} async-done(((bf16[128,16,128]{2,0,1:T(8,128)(2,1)}), bf16[128,16,128]{2,0,1:T(8,128)(2,1)S(1)}, u32[]{:S(2)}, u32[]{:S(2)}) %all-to-all-start.3) | async-done | bytes 524320 | tf_op jit(solution)/shard_map/all_to_all | solution.py:119
  63.6 3.5 %all-to-all-start.7 = ((bf16[128,16,128]{2,0,1:T(8,128)(2,1)}), bf16[128,16,128]{2,0,1:T(8,128)(2,1)S(1)}, u32[]{:S(2)}, u32[]{:S(2)}) async-start(bf16[128,16,128]{2,0,1:T(8,128)(2,1)} %copy.49), calls=%async_computation.7 | async-start | bytes 1048576 | tf_op jit(solution)/shard_map/all_to_all | solution.py:120
  67.1 12.2 %all_gather.12 = s32[1,512]{1,0:T(1,128)S(1)} all-gather(s32[1,128]{1,0:T(1,128)S(1)} %copy-done.4), channel_id=1, replica_groups=mesh['dp'=8,'seq'=4] {'seq'}, dimensions={1}, use_global_device_ids=true | all-gather | bytes 2560 | tf_op jit(solution)/shard_map/all_gather | solution.py:117
  79.7 17.2 %all_gather.11 = bf16[512,4,128]{2,0,1:T(8,128)(2,1)S(1)} all-gather(bf16[128,4,128]{2,0,1:T(8,128)(2,1)S(1)} %copy.41), channel_id=1, replica_groups=mesh['dp'=8,'seq'=4] {'seq'}, dimensions={0}, use_global_device_ids=true | all-gather | bytes 655360 | tf_op jit(solution)/shard_map/all_gather | solution.py:124
  96.9 1.4 gather_fusion
  98.3 15.8 %all_gather.14 = bf16[512,4,128]{2,0,1:T(8,128)(2,1)S(1)} all-gather(bf16[128,4,128]{2,0,1:T(8,128)(2,1)S(1)} %copy.42), channel_id=1, replica_groups=mesh['dp'=8,'seq'=4] {'seq'}, dimensions={0}, use_global_device_ids=true | all-gather | bytes 655360 | tf_op jit(solution)/shard_map/all_gather | solution.py:123
  115.4 0.7 fusion.13
  116.2 2.1 fusion.23
  119.4 1.4 multiply_reduce_fusion
  120.8 0.8 fusion.1
  121.6 1.3 copy-done
  122.9 1.4 fusion.9
  124.3 2.1 copy.54
  126.5 4.1 %all-to-all-start.8 = ((bf16[512,4,128]{2,1,0:T(4,128)(2,1)}), bf16[512,4,128]{2,1,0:T(4,128)(2,1)}, u32[]{:S(2)}, u32[]{:S(2)}) async-start(bf16[512,4,128]{2,1,0:T(4,128)(2,1)} %copy.54), calls=%async_computation.8 | async-start | bytes 1048576 | tf_op jit(solution)/shard_map/all_to_all | solution.py:136
  130.6 2.1 copy.47
  132.7 9.9 %all-to-all-done.8 = bf16[512,4,128]{2,1,0:T(4,128)(2,1)} async-done(((bf16[512,4,128]{2,1,0:T(4,128)(2,1)}), bf16[512,4,128]{2,1,0:T(4,128)(2,1)}, u32[]{:S(2)}, u32[]{:S(2)}) %all-to-all-start.8) | async-done | bytes 524320 | tf_op jit(solution)/shard_map/all_to_all | solution.py:136
  142.6 4.9 %all-to-all-start.4 = ((bf16[512,4,128]{2,1,0:T(4,128)(2,1)}), bf16[512,4,128]{2,1,0:T(4,128)(2,1)}, u32[]{:S(2)}, u32[]{:S(2)}) async-start(bf16[512,4,128]{2,1,0:T(4,128)(2,1)} %copy.47), calls=%async_computation.4 | async-start | bytes 1048576 | tf_op jit(solution)/shard_map/all_to_all | solution.py:135
  147.6 2.0 copy.71
  149.6 2.2 reshape.191
  151.8 6.2 %all-to-all-done.4 = bf16[512,4,128]{2,1,0:T(4,128)(2,1)} async-done(((bf16[512,4,128]{2,1,0:T(4,128)(2,1)}), bf16[512,4,128]{2,1,0:T(4,128)(2,1)}, u32[]{:S(2)}, u32[]{:S(2)}) %all-to-all-start.4) | async-done | bytes 524320 | tf_op jit(solution)/shard_map/all_to_all | solution.py:135
  158.0 6.2 %all-to-all-start.9 = ((bf16[8,16,2048]{2,1,0:T(8,128)(2,1)}), bf16[8,16,2048]{2,1,0:T(8,128)(2,1)}, u32[]{:S(2)}, u32[]{:S(2)}) async-start(bf16[8,16,2048]{2,1,0:T(8,128)(2,1)} %reshape.191), calls=%async_computation.9 | async-start | bytes 1048576 | tf_op jit(solution)/shard_map/all_to_all | solution.py:160
  164.1 2.0 copy.72
  166.2 2.2 reshape.187
  168.4 5.6 %all-to-all-done.9 = bf16[8,16,2048]{2,1,0:T(8,128)(2,1)} async-done(((bf16[8,16,2048]{2,1,0:T(8,128)(2,1)}), bf16[8,16,2048]{2,1,0:T(8,128)(2,1)}, u32[]{:S(2)}, u32[]{:S(2)}) %all-to-all-start.9) | async-done | bytes 524320 | tf_op jit(solution)/shard_map/all_to_all | solution.py:160
  174.0 4.2 %all-to-all-start.5 = ((bf16[8,16,2048]{2,1,0:T(8,128)(2,1)}), bf16[8,16,2048]{2,1,0:T(8,128)(2,1)}, u32[]{:S(2)}, u32[]{:S(2)}) async-start(bf16[8,16,2048]{2,1,0:T(8,128)(2,1)} %reshape.187), calls=%async_computation.5 | async-start | bytes 1048576 | tf_op jit(solution)/shard_map/all_to_all | solution.py:153
  178.1 2.3 fusion.7
  180.5 1.7 copy.56
  182.1 5.8 %all-to-all-done.5 = bf16[8,16,2048]{2,1,0:T(8,128)(2,1)} async-done(((bf16[8,16,2048]{2,1,0:T(8,128)(2,1)}), bf16[8,16,2048]{2,1,0:T(8,128)(2,1)}, u32[]{:S(2)}, u32[]{:S(2)}) %all-to-all-start.5) | async-done | bytes 524320 | tf_op jit(solution)/shard_map/all_to_all | solution.py:153
  187.9 4.2 %all-to-all-start.10 = ((f32[512,4,128]{2,1,0:T(4,128)}), f32[512,4,128]{2,1,0:T(4,128)}, u32[]{:S(2)}, u32[]{:S(2)}) async-start(f32[512,4,128]{2,1,0:T(4,128)} %copy.56), calls=%async_computation.10 | async-start | bytes 2097152 | tf_op jit(solution)/shard_map/all_to_all | solution.py:139
  192.9 1.6 copy.59
  194.5 21.4 %all-to-all-done.10 = f32[512,4,128]{2,1,0:T(4,128)} async-done(((f32[512,4,128]{2,1,0:T(4,128)}), f32[512,4,128]{2,1,0:T(4,128)}, u32[]{:S(2)}, u32[]{:S(2)}) %all-to-all-start.10) | async-done | bytes 1048608 | tf_op jit(solution)/shard_map/all_to_all | solution.py:139
  215.9 3.5 %all-to-all-start.12 = ((f32[512,4,128]{2,1,0:T(4,128)}), f32[512,4,128]{2,1,0:T(4,128)S(1)}, u32[]{:S(2)}, u32[]{:S(2)}) async-start(f32[512,4,128]{2,1,0:T(4,128)} %copy.59), calls=%async_computation.12 | async-start | bytes 2097152 | tf_op jit(solution)/shard_map/all_to_all | solution.py:140
  219.4 1.9 reduce_sum.38
  222.1 22.5 %all-to-all-done.12 = f32[512,4,128]{2,1,0:T(4,128)S(1)} async-done(((f32[512,4,128]{2,1,0:T(4,128)}), f32[512,4,128]{2,1,0:T(4,128)S(1)}, u32[]{:S(2)}, u32[]{:S(2)}) %all-to-all-start.12) | async-done | bytes 1048608 | tf_op jit(solution)/shard_map/all_to_all | solution.py:140
  244.6 4.6 %all-to-all-start.11 = ((bf16[8,16,512]{2,1,0:T(8,128)(2,1)}), bf16[8,16,512]{2,1,0:T(8,128)(2,1)S(1)}, u32[]{:S(2)}, u32[]{:S(2)}) async-start(bf16[8,16,512]{2,1,0:T(8,128)(2,1)} %convert_element_type.61), calls=%async_computation.11 | async-start | bytes 262144 | tf_op jit(solution)/shard_map/all_to_all | solution.py:167
  250.6 4.0 %all-to-all-done.11 = bf16[8,16,512]{2,1,0:T(8,128)(2,1)S(1)} async-done(((bf16[8,16,512]{2,1,0:T(8,128)(2,1)}), bf16[8,16,512]{2,1,0:T(8,128)(2,1)S(1)}, u32[]{:S(2)}, u32[]{:S(2)}) %all-to-all-start.11) | async-done | bytes 131104 | tf_op jit(solution)/shard_map/all_to_all | solution.py:167
  254.7 3.4 %all-to-all-start.13 = ((bf16[8,16,512]{2,1,0:T(8,128)(2,1)}), bf16[8,16,512]{2,1,0:T(8,128)(2,1)S(1)}, u32[]{:S(2)}, u32[]{:S(2)}) async-start(bf16[8,16,512]{2,1,0:T(8,128)(2,1)} %convert_element_type.65), calls=%async_computation.13 | async-start | bytes 262144 | tf_op jit(solution)/shard_map/all_to_all | solution.py:176
  258.1 5.5 %all-to-all-done.13 = bf16[8,16,512]{2,1,0:T(8,128)(2,1)S(1)} async-done(((bf16[8,16,512]{2,1,0:T(8,128)(2,1)}), bf16[8,16,512]{2,1,0:T(8,128)(2,1)S(1)}, u32[]{:S(2)}, u32[]{:S(2)}) %all-to-all-start.13) | async-done | bytes 131104 | tf_op jit(solution)/shard_map/all_to_all | solution.py:176
  263.5 1.9 copy.77
  265.4 1.9 copy.78
  (33 shorter events, 7.1 us)
Async XLA Ops:
  20.1 47.0 %copy-start.4 = (s32[1,128]{1,0:T(1,128)S(1)}, s32[1,128]{1,0:T(1,128)}, u32[]{:S(2)}) copy-start(s32[1,128]{1,0:T(1,128)} %param.19) | copy-start | bytes 1540
  33.4 13.2 %all-to-all-start.6 = ((bf16[8,16,2048]{2,1,0:T(8,128)(2,1)}), bf16[8,16,2048]{2,1,0:T(8,128)(2,1)S(1)}, u32[]{:S(2)}, u32[]{:S(2)}) async-start(bf16[8,16,2048]{2,1,0:T(8,128)(2,1)} %bitcast.95), calls=%async_computation.6 | async-start | bytes 1048576 | tf_op jit(solution)/shard_map/all_to_all | solution.py:105
  46.6 17.0 %all-to-all-start.3 = ((bf16[128,16,128]{2,0,1:T(8,128)(2,1)}), bf16[128,16,128]{2,0,1:T(8,128)(2,1)S(1)}, u32[]{:S(2)}, u32[]{:S(2)}) async-start(bf16[128,16,128]{2,0,1:T(8,128)(2,1)} %copy.43), calls=%async_computation.3 | async-start | bytes 1048576 | tf_op jit(solution)/shard_map/all_to_all | solution.py:119
  63.6 51.3 %all-to-all-start.7 = ((bf16[128,16,128]{2,0,1:T(8,128)(2,1)}), bf16[128,16,128]{2,0,1:T(8,128)(2,1)S(1)}, u32[]{:S(2)}, u32[]{:S(2)}) async-start(bf16[128,16,128]{2,0,1:T(8,128)(2,1)} %copy.49), calls=%async_computation.7 | async-start | bytes 1048576 | tf_op jit(solution)/shard_map/all_to_all | solution.py:120
  114.8 1.3 copy-start.1
  118.3 1.0 copy-start.3
  120.8 2.1 copy-start.2
  121.6 1.3 copy-start
  126.5 16.2 %all-to-all-start.8 = ((bf16[512,4,128]{2,1,0:T(4,128)(2,1)}), bf16[512,4,128]{2,1,0:T(4,128)(2,1)}, u32[]{:S(2)}, u32[]{:S(2)}) async-start(bf16[512,4,128]{2,1,0:T(4,128)(2,1)} %copy.54), calls=%async_computation.8 | async-start | bytes 1048576 | tf_op jit(solution)/shard_map/all_to_all | solution.py:136
  142.6 15.3 %all-to-all-start.4 = ((bf16[512,4,128]{2,1,0:T(4,128)(2,1)}), bf16[512,4,128]{2,1,0:T(4,128)(2,1)}, u32[]{:S(2)}, u32[]{:S(2)}) async-start(bf16[512,4,128]{2,1,0:T(4,128)(2,1)} %copy.47), calls=%async_computation.4 | async-start | bytes 1048576 | tf_op jit(solution)/shard_map/all_to_all | solution.py:135
  158.0 16.0 %all-to-all-start.9 = ((bf16[8,16,2048]{2,1,0:T(8,128)(2,1)}), bf16[8,16,2048]{2,1,0:T(8,128)(2,1)}, u32[]{:S(2)}, u32[]{:S(2)}) async-start(bf16[8,16,2048]{2,1,0:T(8,128)(2,1)} %reshape.191), calls=%async_computation.9 | async-start | bytes 1048576 | tf_op jit(solution)/shard_map/all_to_all | solution.py:160
  174.0 13.9 %all-to-all-start.5 = ((bf16[8,16,2048]{2,1,0:T(8,128)(2,1)}), bf16[8,16,2048]{2,1,0:T(8,128)(2,1)}, u32[]{:S(2)}, u32[]{:S(2)}) async-start(bf16[8,16,2048]{2,1,0:T(8,128)(2,1)} %reshape.187), calls=%async_computation.5 | async-start | bytes 1048576 | tf_op jit(solution)/shard_map/all_to_all | solution.py:153
  187.9 28.0 %all-to-all-start.10 = ((f32[512,4,128]{2,1,0:T(4,128)}), f32[512,4,128]{2,1,0:T(4,128)}, u32[]{:S(2)}, u32[]{:S(2)}) async-start(f32[512,4,128]{2,1,0:T(4,128)} %copy.56), calls=%async_computation.10 | async-start | bytes 2097152 | tf_op jit(solution)/shard_map/all_to_all | solution.py:139
  215.9 28.7 %all-to-all-start.12 = ((f32[512,4,128]{2,1,0:T(4,128)}), f32[512,4,128]{2,1,0:T(4,128)S(1)}, u32[]{:S(2)}, u32[]{:S(2)}) async-start(f32[512,4,128]{2,1,0:T(4,128)} %copy.59), calls=%async_computation.12 | async-start | bytes 2097152 | tf_op jit(solution)/shard_map/all_to_all | solution.py:140
  244.6 10.1 %all-to-all-start.11 = ((bf16[8,16,512]{2,1,0:T(8,128)(2,1)}), bf16[8,16,512]{2,1,0:T(8,128)(2,1)S(1)}, u32[]{:S(2)}, u32[]{:S(2)}) async-start(bf16[8,16,512]{2,1,0:T(8,128)(2,1)} %convert_element_type.61), calls=%async_computation.11 | async-start | bytes 262144 | tf_op jit(solution)/shard_map/all_to_all | solution.py:167
  254.7 8.8 %all-to-all-start.13 = ((bf16[8,16,512]{2,1,0:T(8,128)(2,1)}), bf16[8,16,512]{2,1,0:T(8,128)(2,1)S(1)}, u32[]{:S(2)}, u32[]{:S(2)}) async-start(bf16[8,16,512]{2,1,0:T(8,128)(2,1)} %convert_element_type.65), calls=%async_computation.13 | async-start | bytes 262144 | tf_op jit(solution)/shard_map/all_to_all | solution.py:176
where the time goes:
time: 270 us; the launch traced here: 269 us
  waiting for transfers between devices  101 us (37%)
  blocking collectives  78.1 us (29%)
  starting transfers between devices  47 us (17%)
  local copies, waits for them, and re-layouts  29.2 us (11%)
  matrix products  7.36 us (3%)
  other arithmetic  5.55 us (2%)
    all_to_all x1, waiting for transfers between devices, shards(): lax.all_to_all(value_gradient, 'seq', split_axis=0, concat_axis=1, tiled=...  22.5 us
    all_to_all x1, waiting for transfers between devices, shards(): lax.all_to_all(key_gradient, 'seq', split_axis=0, concat_axis=1, tiled=True)  21.4 us
    all_gather x1, blocking collectives, shards(): lax.all_gather(value_tokens, 'seq', axis=0, tiled=True)  17.2 us
    all_gather x1, blocking collectives, shards(): lax.all_gather(key_tokens, 'seq', axis=0, tiled=True)  15.8 us
    all_to_all x1, blocking collectives, shards(): lax.all_to_all(queries.reshape(group_count, packed_slab_rows, QUERY_HEADS...  13.3 us
    all_gather x1, blocking collectives, shards(): doc_row = lax.all_gather(doc_ids, 'seq', axis=1, tiled=True)[0]  12.2 us
    all_to_all x1, waiting for transfers between devices, shards(): lax.all_to_all(query_tok, 'seq', split_axis=1, concat_axis=0, tiled=True)  11.1 us
    all_to_all x1, blocking collectives, shards(): lax.all_to_all(keys.reshape(group_count, packed_slab_rows, KEY_VALUE_HEAD...  10.7 us
  transfers between devices with their start and end apart: 11, of which 10 were waited for; matrix products, arithmetic and copies ran while one was open for 10% of the time, Pallas kernels for 0%

commit v1 on v0

--- a/solution.py
+++ b/solution.py
@@ -1,8 +1,11 @@
+import functools
 import math
 
 import jax
 import jax.numpy as jnp
 from jax import lax
+from jax.experimental import pallas as pl
+from jax.experimental.pallas import tpu as pltpu
 from jax.sharding import PartitionSpec as P
 
 QUERY_HEADS = 16
@@ -191,6 +194,461 @@
     )
 
 
+MESH = pl.DeviceIdType.MESH
+SLAB = 16
+ROWS = 8
+CHUNKS = 4
+CHUNK_ROWS = ROWS // CHUNKS
+REACH = 2
+SLOTS = 2 * REACH + 2
+WINDOW = SLOTS * SLAB
+HALF_Q = QUERY_HEADS * HEAD_DIMENSION // 2
+HALF_K = KEY_VALUE_HEADS * HEAD_DIMENSION // 2
+GROUP = QUERY_HEADS // KEY_VALUE_HEADS
+SCALING = 1.0 / math.sqrt(HEAD_DIMENSION)
+MASKED = -1e30
+
+
+def kernel(
+    n_dp, n_seq, q, k, v, u, doc, att, dq, dk, dv,
+    qb, ub, kw, vw, ob, gb, kg, vg, kp, vp, ks, vs, docs, dwin, bias,
+    doc_send, doc_recv, doc_local, fwd_send, fwd_recv, half_send, half_recv, local_in,
+    back_send, back_recv, out_send, out_recv, local_out, final_out,
+):
+    d = lax.axis_index("dp")
+    z = lax.axis_index("seq")
+    chip, s = d // 2, d % 2
+    chips = n_dp // 2
+    place = z * chips + chip
+    last = n_seq * chips - 1
+    before, after = (z + n_seq - 1) % n_seq, (z + 1) % n_seq
+    sibling = (chip * 2 + 1 - s, z)
+
+    def remote(src, dst, send, recv, device):
+        return pltpu.make_async_remote_copy(
+            src_ref=src, dst_ref=dst, send_sem=send, recv_sem=recv,
+            device_id=device, device_id_type=MESH,
+        )
+
+    def device_at(where, core):
+        inside = (where + n_seq * chips) % (n_seq * chips)
+        return ((inside % chips) * 2 + core, inside // chips)
+
+    barrier = pltpu.get_barrier_semaphore()
+    for step in range(1, n_dp):
+        pl.semaphore_signal(barrier, inc=1, device_id=((d + step) % n_dp, z), device_id_type=MESH)
+
+    @pl.when(z > 0)
+    def _():
+        for other in range(n_dp):
+            pl.semaphore_signal(barrier, inc=1, device_id=(other, before), device_id_type=MESH)
+
+    @pl.when(z < n_seq - 1)
+    def _():
+        for other in range(n_dp):
+            pl.semaphore_signal(barrier, inc=1, device_id=(other, after), device_id_type=MESH)
+
+    planes = (z > 0).astype(jnp.int32) + (z < n_seq - 1).astype(jnp.int32)
+    own_cols = pl.ds(pl.multiple_of(s * HALF_Q, HALF_Q), HALF_Q)
+    sib_cols = pl.ds(pl.multiple_of((1 - s) * HALF_Q, HALF_Q), HALF_Q)
+    own_kcols = pl.ds(pl.multiple_of(s * HALF_K, HALF_K), HALF_K)
+    sib_kcols = pl.ds(pl.multiple_of((1 - s) * HALF_K, HALF_K), HALF_K)
+
+    def rows_of(chunk):
+        return pl.ds(chunk * CHUNK_ROWS, CHUNK_ROWS)
+
+    def local_in_copies(chunk):
+        rows = rows_of(chunk)
+        return [
+            pltpu.make_async_copy(k.at[rows, :, own_kcols], kw.at[rows, 2 * REACH + s], local_in.at[chunk, 0]),
+            pltpu.make_async_copy(v.at[rows, :, own_kcols], vw.at[rows, 2 * REACH + s], local_in.at[chunk, 1]),
+            pltpu.make_async_copy(q.at[rows, :, own_cols], qb.at[rows, s], local_in.at[chunk, 2]),
+            pltpu.make_async_copy(u.at[rows, :, own_cols], ub.at[rows, s], local_in.at[chunk, 3]),
+        ]
+
+    own_doc = pltpu.make_async_copy(doc, docs.at[n_dp + d], doc_local)
+    own_doc.start()
+    for chunk in range(CHUNKS):
+        for copy in local_in_copies(chunk):
+            copy.start()
+
+    for offset in range(1, REACH + 1):
+
+        @pl.when(place < offset)
+        def _():
+            for core in range(2):
+                slot = 2 * (REACH - offset) + core
+                kw[:, slot] = jnp.zeros((ROWS, SLAB, HALF_K), jnp.bfloat16)
+                vw[:, slot] = jnp.zeros((ROWS, SLAB, HALF_K), jnp.bfloat16)
+
+        @pl.when(place + offset > last)
+        def _():
+            kp[offset] = jnp.zeros((ROWS, SLAB, 2 * HALF_K), jnp.bfloat16)
+            vp[offset] = jnp.zeros((ROWS, SLAB, 2 * HALF_K), jnp.bfloat16)
+
+    @pl.when(z == 0)
+    def _():
+        docs[0:n_dp] = jnp.zeros((n_dp, 1, n_dp * SLAB), jnp.int32)
+
+    pl.semaphore_wait(barrier, n_dp - 1 + n_dp * planes)
+
+    def doc_near(step):
+        return remote(
+            doc, docs.at[n_dp + d], doc_send.at[step], doc_recv.at[n_dp + d], ((d + step) % n_dp, z)
+        )
+
+    def doc_next(other):
+        return remote(
+            doc, docs.at[d], doc_send.at[n_dp + other], doc_recv.at[d], (other, after)
+        )
+
+    for step in range(1, n_dp):
+        doc_near(step).start()
+
+    @pl.when(z < n_seq - 1)
+    def _():
+        for other in range(n_dp):
+            doc_next(other).start()
+
+    def forward(chunk, kind, offset, core):
+        src, dst = ((k, kw), (v, vw))[kind]
+        rows = rows_of(chunk)
+        columns = pl.ds(core * HALF_K, HALF_K)
+        return remote(
+            src.at[rows, :, columns],
+            dst.at[rows, 2 * (REACH - offset) + s],
+            fwd_send.at[chunk, kind, 2 * offset + core],
+            fwd_recv.at[chunk, kind, 2 * (REACH - offset) + s],
+            device_at(place + offset, core),
+        )
+
+    def forward_sibling(chunk, kind):
+        src, dst = ((k, kw), (v, vw))[kind]
+        rows = rows_of(chunk)
+        return remote(
+            src.at[rows, :, sib_kcols],
+            dst.at[rows, 2 * REACH + s],
+            fwd_send.at[chunk, kind, 0],
+            fwd_recv.at[chunk, kind, 2 * REACH + s],
+            sibling,
+        )
+
+    def half_over(chunk, kind):
+        src, dst = ((q, qb), (u, ub))[kind]
+        rows = rows_of(chunk)
+        return remote(
+            src.at[rows, :, sib_cols], dst.at[rows, s],
+            half_send.at[chunk, kind], half_recv.at[chunk, kind], sibling,
+        )
+
+    def send_forward(chunk, act):
+        for offset in range(REACH, 0, -1):
+
+            @pl.when(place + offset <= last)
+            def _():
+                for kind in range(2):
+                    for core in range(2):
+                        act(forward(chunk, kind, offset, core))
+
+        for kind in range(2):
+            act(forward_sibling(chunk, kind))
+            act(half_over(chunk, kind))
+
+    for chunk in range(CHUNKS):
+        send_forward(chunk, lambda copy: copy.start())
+
+    own_doc.wait()
+    for step in range(1, n_dp):
+        other = (d + step) % n_dp
+        pltpu.make_async_copy(doc, docs.at[n_dp + other], doc_recv.at[n_dp + other]).wait()
+
+    @pl.when(z > 0)
+    def _():
+        for other in range(n_dp):
+            pltpu.make_async_copy(doc, docs.at[other], doc_recv.at[other]).wait()
+
+    for row in range(n_dp):
+        dwin[row : row + 1, 0:128] = docs[row]
+        dwin[row : row + 1, 128:256] = docs[n_dp + row]
+    lead = 128 - 2 * REACH * SLAB
+    both = dwin[...]
+    window = jnp.zeros((n_dp, 128), jnp.int32)
+    for candidate in range(chips):
+        begin = lead + candidate * 2 * SLAB
+        shifted = pltpu.roll(both, 256 - begin, axis=1)[:, :128]
+        window = jnp.where(chip == candidate, shifted, window)
+    own = window[:, 2 * REACH * SLAB : WINDOW]
+    query_docs = jnp.concatenate([own] * GROUP, axis=1)
+    key_docs = window.astype(jnp.float32).T[:WINDOW]
+    key_at = lax.broadcasted_iota(jnp.int32, (WINDOW, 128), 0)
+    query_at = lax.broadcasted_iota(jnp.int32, (WINDOW, 128), 1) % (2 * SLAB) + 2 * REACH * SLAB
+    in_order = (key_at <= query_at) & (key_at >= 2 * REACH * SLAB - place * 2 * SLAB)
+    query_docs = query_docs.astype(jnp.float32)
+    for row in range(n_dp):
+        same = key_docs[:, row : row + 1] == query_docs[row : row + 1, :]
+        bias[row] = jnp.where(same & in_order, 0.0, MASKED)
+
+    def backward(chunk, kind, offset, core):
+        src, dst = ((kg, kp), (vg, vp))[kind]
+        rows = rows_of(chunk)
+        return remote(
+            src.at[rows, 2 * (REACH - offset) + core],
+            dst.at[offset, rows, :, own_kcols],
+            back_send.at[chunk, kind, 2 * offset + core],
+            back_recv.at[chunk, kind, 2 * offset + s],
+            device_at(place - offset, core),
+        )
+
+    def backward_sibling(chunk, kind):
+        src, dst = ((kg, kp), (vg, vp))[kind]
+        rows = rows_of(chunk)
+        return remote(
+            src.at[rows, 2 * REACH + 1 - s],
+            dst.at[0, rows, :, own_kcols],
+            back_send.at[chunk, kind, 0],
+            back_recv.at[chunk, kind, s],
+            sibling,
+        )
+
+    def out_over(chunk, kind):
+        src, dst = ((ob, att), (gb, dq))[kind]
+        rows = rows_of(chunk)
+        return remote(
+            src.at[rows, 1 - s], dst.at[rows, :, own_cols],
+            out_send.at[chunk, kind], out_recv.at[chunk, kind], sibling,
+        )
+
+    def local_out_copy(chunk, which):
+        rows = rows_of(chunk)
+        if which < 2:
+            src, dst = ((kg, kp), (vg, vp))[which]
+            return pltpu.make_async_copy(
+                src.at[rows, 2 * REACH + s], dst.at[0, rows, :, own_kcols], local_out.at[chunk, which]
+            )
+        src, dst = ((ob, att), (gb, dq))[which - 2]
+        return pltpu.make_async_copy(
+            src.at[rows, s], dst.at[rows, :, own_cols], local_out.at[chunk, which]
+        )
+
+    def send_backward(chunk, act):
+        for offset in range(REACH, 0, -1):
+
+            @pl.when(place - offset >= 0)
+            def _():
+                for kind in range(2):
+                    for core in range(2):
+                        act(backward(chunk, kind, offset, core))
+
+        for kind in range(2):
+            act(backward_sibling(chunk, kind))
+            act(out_over(chunk, kind))
+
+    def await_inputs(chunk):
+        rows = rows_of(chunk)
+        for copy in local_in_copies(chunk):
+            copy.wait()
+        for kind in range(2):
+            src, dst = ((k, kw), (v, vw))[kind]
+            slot = 2 * REACH + 1 - s
+            pltpu.make_async_copy(
+                src.at[rows, :, own_kcols], dst.at[rows, slot], fwd_recv.at[chunk, kind, slot]
+            ).wait()
+            src, dst = ((q, qb), (u, ub))[kind]
+            pltpu.make_async_copy(
+                src.at[rows, :, own_cols], dst.at[rows, 1 - s], half_recv.at[chunk, kind]
+            ).wait()
+        for offset in range(1, REACH + 1):
+
+            @pl.when(place >= offset)
+            def _():
+                for kind in range(2):
+                    src, dst = ((k, kw), (v, vw))[kind]
+                    for core in range(2):
+                        slot = 2 * (REACH - offset) + core
+                        pltpu.make_async_copy(
+                            src.at[rows, :, own_kcols], dst.at[rows, slot], fwd_recv.at[chunk, kind, slot]
+                        ).wait()
+
+    def dot(a, b, dims):
+        return lax.dot_general(a, b, (dims, ((), ())), preferred_element_type=jnp.float32)
+
+    def compute(chunk):
+        tasks = [(i, g) for i in range(CHUNK_ROWS) for g in range(2)]
+        first = chunk * CHUNK_ROWS
+
+        def stacked(ref, i, g):
+            parts = []
+            for h in range(GROUP):
+                at = (g * GROUP + h) * HEAD_DIMENSION
+                parts.append(ref[first + i, :, :, at : at + HEAD_DIMENSION].reshape(2 * SLAB, HEAD_DIMENSION))
+            return jnp.concatenate(parts, axis=0)
+
+        def windowed(ref, i, g):
+            at = g * HEAD_DIMENSION
+            return ref[first + i, :, :, at : at + HEAD_DIMENSION].reshape(WINDOW, HEAD_DIMENSION)
+
+        def spread(ref, i, g, value):
+            for h in range(GROUP):
+                at = (g * GROUP + h) * HEAD_DIMENSION
+                part = value[h * 2 * SLAB : (h + 1) * 2 * SLAB].astype(jnp.bfloat16)
+                ref[first + i, :, :, at : at + HEAD_DIMENSION] = part.reshape(2, SLAB, HEAD_DIMENSION)
+
+        def unwindow(ref, i, g, value):
+            at = g * HEAD_DIMENSION
+            ref[first + i, :, :, at : at + HEAD_DIMENSION] = value.astype(jnp.bfloat16).reshape(
+                SLOTS, SLAB, HEAD_DIMENSION
+            )
+
+        scores = [dot(windowed(kw, i, g), stacked(qb, i, g), ((1,), (1,))) for i, g in tasks]
+        prob_grads = [dot(windowed(vw, i, g), stacked(ub, i, g), ((1,), (1,))) for i, g in tasks]
+        probs, grads = [], []
+        for (i, g), score, prob_grad in zip(tasks, scores, prob_grads):
+            score = score * SCALING + bias[first + i]
+            weights = jnp.exp(score - jnp.max(score, axis=0, keepdims=True))
+            normalized = weights / jnp.sum(weights, axis=0, keepdims=True)
+            delta = jnp.sum(normalized * prob_grad, axis=0, keepdims=True)
+            probs.append(normalized.astype(jnp.bfloat16))
+            grads.append((normalized * (prob_grad - delta)).astype(jnp.bfloat16))
+        for (i, g), prob, grad in zip(tasks, probs, grads):
+            unwindow(kg, i, g, dot(grad, stacked(qb, i, g), ((1,), (0,))) * SCALING)
+            unwindow(vg, i, g, dot(prob, stacked(ub, i, g), ((1,), (0,))))
+        for (i, g), prob, grad in zip(tasks, probs, grads):
+            spread(ob, i, g, dot(prob, windowed(vw, i, g), ((0,), (0,))))
+            spread(gb, i, g, dot(grad, windowed(kw, i, g), ((0,), (0,))) * SCALING)
+
+    def step(chunk, carry):
+        await_inputs(chunk)
+        compute(chunk)
+        send_backward(chunk, lambda copy: copy.start())
+        for which in range(4):
+            local_out_copy(chunk, which).start()
+        return carry
+
+    lax.fori_loop(0, CHUNKS, step, 0)
+
+    def finish(chunk, carry):
+        rows = rows_of(chunk)
+        for kind in range(2):
+            local_out_copy(chunk, kind).wait()
+            src, dst = ((kg, kp), (vg, vp))[kind]
+            pltpu.make_async_copy(
+                src.at[rows, 2 * REACH + 1 - s], dst.at[0, rows, :, sib_kcols], back_recv.at[chunk, kind, 1 - s]
+            ).wait()
+        for offset in range(1, REACH + 1):
+
+            @pl.when(place + offset <= last)
+            def _():
+                for kind in range(2):
+                    src, dst = ((kg, kp), (vg, vp))[kind]
+                    for core in range(2):
+                        pltpu.make_async_copy(
+                            src.at[rows, 2 * REACH],
+                            dst.at[offset, rows, :, pl.ds(core * HALF_K, HALF_K)],
+                            back_recv.at[chunk, kind, 2 * offset + core],
+                        ).wait()
+
+        for part, total, target, kind in ((kp, ks, dk, 0), (vp, vs, dv, 1)):
+            value = part[0, rows].astype(jnp.float32)
+            for offset in range(1, REACH + 1):
+                value += part[offset, rows].astype(jnp.float32)
+            total[rows] = value.astype(jnp.bfloat16)
+            pltpu.make_async_copy(total.at[rows], target.at[rows], final_out.at[chunk, kind]).start()
+        return carry
+
+    lax.fori_loop(0, CHUNKS, finish, 0)
+
+    for step in range(1, n_dp):
+        doc_near(step).wait_send()
+
+    @pl.when(z < n_seq - 1)
+    def _():
+        for other in range(n_dp):
+            doc_next(other).wait_send()
+
+    def drain(chunk, carry):
+        rows = rows_of(chunk)
+        send_forward(chunk, lambda copy: copy.wait_send())
+        send_backward(chunk, lambda copy: copy.wait_send())
+        for kind in range(2):
+            src, dst = ((ob, att), (gb, dq))[kind]
+            pltpu.make_async_copy(
+                src.at[rows, s], dst.at[rows, :, sib_cols], out_recv.at[chunk, kind]
+            ).wait()
+            local_out_copy(chunk, 2 + kind).wait()
+            total, target = ((ks, dk), (vs, dv))[kind]
+            pltpu.make_async_copy(total.at[rows], target.at[rows], final_out.at[chunk, kind]).wait()
+        return carry
+
+    lax.fori_loop(0, CHUNKS, drain, 0)
+
+
+def direct(n_dp, n_seq, queries, keys, values, upstream, doc_ids):
+    wide = (ROWS, SLAB, QUERY_HEADS * HEAD_DIMENSION)
+    narrow = (ROWS, SLAB, KEY_VALUE_HEADS * HEAD_DIMENSION)
+    half = jnp.bfloat16
+    anywhere = pl.BlockSpec(memory_space=pl.ANY)
+    dma = pltpu.SemaphoreType.DMA
+    results = pl.pallas_call(
+        functools.partial(kernel, n_dp, n_seq),
+        out_shape=[jax.ShapeDtypeStruct(shape, half) for shape in (wide, wide, narrow, narrow)],
+        in_specs=[anywhere] * 5,
+        out_specs=[anywhere] * 4,
+        scratch_shapes=[
+            pltpu.VMEM((ROWS, 2, SLAB, HALF_Q), half),
+            pltpu.VMEM((ROWS, 2, SLAB, HALF_Q), half),
+            pltpu.VMEM((ROWS, SLOTS, SLAB, HALF_K), half),
+            pltpu.VMEM((ROWS, SLOTS, SLAB, HALF_K), half),
+            pltpu.VMEM((ROWS, 2, SLAB, HALF_Q), half),
+            pltpu.VMEM((ROWS, 2, SLAB, HALF_Q), half),
+            pltpu.VMEM((ROWS, SLOTS, SLAB, HALF_K), half),
+            pltpu.VMEM((ROWS, SLOTS, SLAB, HALF_K), half),
+            pltpu.VMEM((REACH + 1,) + narrow, half),
+            pltpu.VMEM((REACH + 1,) + narrow, half),
+            pltpu.VMEM(narrow, half),
+            pltpu.VMEM(narrow, half),
+            pltpu.VMEM((2 * n_dp, 1, n_dp * SLAB), jnp.int32),
+            pltpu.VMEM((n_dp, 2 * n_dp * SLAB), jnp.int32),
+            pltpu.VMEM((ROWS, WINDOW, 128), jnp.float32),
+            dma((2 * n_dp,)),
+            dma((2 * n_dp,)),
+            dma(()),
+            dma((CHUNKS, 2, SLOTS)),
+            dma((CHUNKS, 2, SLOTS)),
+            dma((CHUNKS, 2)),
+            dma((CHUNKS, 2)),
+            dma((CHUNKS, 4)),
+            dma((CHUNKS, 2, SLOTS)),
+            dma((CHUNKS, 2, SLOTS)),
+            dma((CHUNKS, 2)),
+            dma((CHUNKS, 2)),
+            dma((CHUNKS, 4)),
+            dma((CHUNKS, 2)),
+        ],
+        compiler_params=pltpu.CompilerParams(
+            collective_id=0, has_side_effects=True, vmem_limit_bytes=48 * 1024 * 1024
+        ),
+        cost_estimate=pl.CostEstimate(flops=10**9, bytes_accessed=10**7, transcendentals=10**6),
+    )(
+        queries.reshape(wide), keys.reshape(narrow), values.reshape(narrow),
+        upstream.reshape(wide), doc_ids,
+    )
+    tokens = ROWS * SLAB
+    return tuple(array.reshape(1, tokens, array.shape[-1]) for array in results)
+
+
+def arranged(n_dp, n_seq, queries, keys, values, upstream, doc_ids):
+    tokens = queries.shape[1]
+    slab = tokens // n_dp
+    longest = n_seq * tokens // 8
+    if n_dp == ROWS and slab == SLAB and longest <= 2 * REACH * SLAB:
+        return direct(n_dp, n_seq, queries, keys, values, upstream, doc_ids)
+    return shards(queries, keys, values, upstream, doc_ids)
+
+
+def pick(mesh):
+    return functools.partial(arranged, mesh.shape["dp"], mesh.shape["seq"])
+
+
 def solution(mesh):
     in_specs = (
         P("dp", "seq", None),
@@ -205,4 +663,5 @@
         P("dp", "seq", None),
         P("dp", "seq", None),
     )
-    return jax.shard_map(shards, mesh=mesh, in_specs=in_specs, out_specs=out_specs, check_vma=False)
+    return jax.shard_map(
+        pick(mesh), mesh=mesh, in_specs=in_specs, out_specs=out_specs, check_vma=False)

time: 270 us -> 37.6 us (0.14)
  waiting for transfers between devices: 101 us -> 0 us
  blocking collectives: 78.1 us -> 0 us
  starting transfers between devices: 47 us -> 0 us
  Pallas kernels: 0 us -> 29.2 us
  local copies, waits for them, and re-layouts: 29.2 us -> 7.44 us
  matrix products: 7.36 us -> 0 us
  other arithmetic: 5.55 us -> 0 us
    all_to_all x11 -> x0, waiting for transfers between devices: 101 us -> none  [the longest x1 22.5 us: shards(): lax.all_to_all(value_gradient, 'seq', split_axis=0, concat_axis=1, tiled=...]
    all_to_all x11 -> x0, starting transfers between devices: 47 us -> none  [the longest x1 6.17 us: shards(): lax.all_to_all(query_back.reshape(group_count, packed_slab_rows, QUERY_HE...]
    all_gather x3 -> x0, blocking collectives: 45.3 us -> none  [the longest x1 17.2 us: shards(): lax.all_gather(value_tokens, 'seq', axis=0, tiled=True)]
    all_to_all x3 -> x0, blocking collectives: 32.8 us -> none  [the longest x1 13.3 us: shards(): lax.all_to_all(queries.reshape(group_count, packed_slab_rows, QUERY_HEADS...]
    pallas_call x0 -> x1, Pallas kernels: none -> 29.2 us  [direct(): pl.pallas_call(functools.partial(kernel, n_dp, n_seq), out_shape=[jax.Sha...]
    dot_general x6 -> x0, matrix products: 7.36 us -> none  [the longest x1 2.3 us: attend(): jnp.einsum('hqk,qhd->khd', score_grad, query_block, preferred_element_typ...]
    reshape x8 -> x0, local copies, waits for them, and re-layouts: 6.42 us -> none  [the longest x1 2.22 us: shards(): query_back.reshape(group_count, packed_slab_rows, QUERY_HEADS * HEAD_DIME...]
    convert_element_type x6 -> x0, local copies, waits for them, and re-layouts: 5.85 us -> none  [the longest x1 2.11 us: attend(): query_parts.append((jnp.einsum('hqk,khd->qhd', score_grad, key_part, pref...]
  transfers between devices with their start and end apart: 11 -> 0, of which waited for: 10 -> 0; matrix products, arithmetic and copies ran while one was open for 10% -> 0% of each run, Pallas kernels for 0% -> 0%
where the time goes in v1:
time: 37.6 us; the launch traced here: 37.3 us
  Pallas kernels  29.2 us (78%)
  local copies, waits for them, and re-layouts  7.44 us (20%)
  between operations  0.65 us (2%)
    pallas_call x1, Pallas kernels, direct(): pl.pallas_call(functools.partial(kernel, n_dp, n_seq), out_shape=[jax.Sha...  29.2 us
    unnamed x14, local copies, waits for them, and re-layouts  7.44 us

profile of v1, /device:TPU:0, one launch (start us, length us, event | category | flops | bytes accessed | tf_op | source)
XLA Modules:
  0.0 37.3 jit_solution(14304776282733438982)
XLA Ops:
  0.6 0.0 copy-start.4
  0.6 0.6 %copy-done.4 = s32[1,128]{1,0:T(1,128)S(1)} copy-done((s32[1,128]{1,0:T(1,128)S(1)}, s32[1,128]{1,0:T(1,128)}, u32[]{:S(2)}) %copy-start.4) | copy-done | bytes 536
  1.3 0.0 copy-start
  1.3 1.0 %copy-done = bf16[1,128,2048]{2,1,0:T(8,128)(2,1)S(1)} copy-done((bf16[1,128,2048]{2,1,0:T(8,128)(2,1)S(1)}, bf16[1,128,2048]{2,1,0:T(8,128)(2,1)}, u32[]{:S(2)}) %copy-start) | copy-done | bytes 524312
  2.3 0.0 copy-start.1
  2.3 1.0 %copy-done.1 = bf16[1,128,2048]{2,1,0:T(8,128)(2,1)S(1)} copy-done((bf16[1,128,2048]{2,1,0:T(8,128)(2,1)S(1)}, bf16[1,128,2048]{2,1,0:T(8,128)(2,1)}, u32[]{:S(2)}) %copy-start.1) | copy-done | bytes 524312
  3.4 0.0 copy-start.2
  3.4 0.9 %copy-done.2 = bf16[1,128,512]{2,1,0:T(8,128)(2,1)S(1)} copy-done((bf16[1,128,512]{2,1,0:T(8,128)(2,1)S(1)}, bf16[1,128,512]{2,1,0:T(8,128)(2,1)}, u32[]{:S(2)}) %copy-start.2) | copy-done | bytes 131096
  4.3 0.0 copy-start.3
  4.3 0.9 %copy-done.3 = bf16[1,128,512]{2,1,0:T(8,128)(2,1)S(1)} copy-done((bf16[1,128,512]{2,1,0:T(8,128)(2,1)S(1)}, bf16[1,128,512]{2,1,0:T(8,128)(2,1)}, u32[]{:S(2)}) %copy-start.3) | copy-done | bytes 131096
  5.2 29.2 %shard_map.84 = (bf16[8,16,2048]{2,1,0:T(8,128)(2,1)S(1)}, bf16[8,16,2048]{2,1,0:T(8,128)(2,1)S(1)}, bf16[8,16,512]{2,1,0:T(8,128)(2,1)S(1)}, bf16[8,16,512]{2,1,0:T(8,128)(2,1)S(1)}) custom-call(bf16[8,16,2048]{2,1,0:T(8,128)(2,1)S(1)} %bitcast.12, bf16[8,16,512]{2,1,0:T(8,128)(2,1)S(1)} %bitcast.14, bf16[8,16,512]{2,1,0:T(8,128)(2,1)S(1)} %bitcast.15, ...), custom_call_target="tpu_custom_call" | custom-call | flops 1000000000 | bytes 10000000 | tf_op jit(solution)/shard_map/pallas_call | solution.py:591
  34.4 0.8 %copy.13 = bf16[1,128,2048]{2,1,0:T(8,128)(2,1)} copy(bf16[1,128,2048]{2,1,0:T(8,128)(2,1)S(1)} %bitcast.9) | data formatting | bytes 1048576
  35.2 0.8 %copy.14 = bf16[1,128,2048]{2,1,0:T(8,128)(2,1)} copy(bf16[1,128,2048]{2,1,0:T(8,128)(2,1)S(1)} %bitcast.8) | data formatting | bytes 1048576
  36.0 0.7 %copy.15 = bf16[1,128,512]{2,1,0:T(8,128)(2,1)} copy(bf16[1,128,512]{2,1,0:T(8,128)(2,1)S(1)} %bitcast.11) | data formatting | bytes 262144
  36.7 0.7 %copy.16 = bf16[1,128,512]{2,1,0:T(8,128)(2,1)} copy(bf16[1,128,512]{2,1,0:T(8,128)(2,1)S(1)} %bitcast.10) | data formatting | bytes 262144
Async XLA Ops:
  0.6 0.7 %copy-start.4 = (s32[1,128]{1,0:T(1,128)S(1)}, s32[1,128]{1,0:T(1,128)}, u32[]{:S(2)}) copy-start(s32[1,128]{1,0:T(1,128)} %doc.1) | copy-start | bytes 1540
  1.3 1.0 %copy-start = (bf16[1,128,2048]{2,1,0:T(8,128)(2,1)S(1)}, bf16[1,128,2048]{2,1,0:T(8,128)(2,1)}, u32[]{:S(2)}) copy-start(bf16[1,128,2048]{2,1,0:T(8,128)(2,1)} %param.5) | copy-start | bytes 1572868
  2.3 1.0 %copy-start.1 = (bf16[1,128,2048]{2,1,0:T(8,128)(2,1)S(1)}, bf16[1,128,2048]{2,1,0:T(8,128)(2,1)}, u32[]{:S(2)}) copy-start(bf16[1,128,2048]{2,1,0:T(8,128)(2,1)} %param.8) | copy-start | bytes 1572868
  3.4 0.9 %copy-start.2 = (bf16[1,128,512]{2,1,0:T(8,128)(2,1)S(1)}, bf16[1,128,512]{2,1,0:T(8,128)(2,1)}, u32[]{:S(2)}) copy-start(bf16[1,128,512]{2,1,0:T(8,128)(2,1)} %param.6) | copy-start | bytes 393220
  4.3 0.9 %copy-start.3 = (bf16[1,128,512]{2,1,0:T(8,128)(2,1)S(1)}, bf16[1,128,512]{2,1,0:T(8,128)(2,1)}, u32[]{:S(2)}) copy-start(bf16[1,128,512]{2,1,0:T(8,128)(2,1)} %param.7) | copy-start | bytes 393220

commit v2 on v1

--- a/solution.py
+++ b/solution.py
@@ -198,6 +198,7 @@
 SLAB = 16
 ROWS = 8
 CHUNKS = 4
+AHEAD = 2
 CHUNK_ROWS = ROWS // CHUNKS
 REACH = 2
 SLOTS = 2 * REACH + 2
@@ -210,9 +211,9 @@
 
 
 def kernel(
-    n_dp, n_seq, q, k, v, u, doc, att, dq, dk, dv,
-    qb, ub, kw, vw, ob, gb, kg, vg, kp, vp, ks, vs, docs, dwin, bias,
-    doc_send, doc_recv, doc_local, fwd_send, fwd_recv, half_send, half_recv, local_in,
+    n_dp, n_seq, q_in, k_in, v_in, u_in, doc_in, att, dq, dk, dv,
+    q, k, v, u, doc, qb, ub, kw, vw, ob, gb, kg, vg, kp, vp, ks, vs, docs, dwin, bias,
+    staged, doc_send, doc_recv, doc_local, fwd_send, fwd_recv, half_send, half_recv, local_in,
     back_send, back_recv, out_send, out_recv, local_out, final_out,
 ):
     d = lax.axis_index("dp")
@@ -234,6 +235,13 @@
         inside = (where + n_seq * chips) % (n_seq * chips)
         return ((inside % chips) * 2 + core, inside // chips)
 
+    stages = [
+        pltpu.make_async_copy(src, dst, staged.at[i])
+        for i, (src, dst) in enumerate(((doc_in, doc), (k_in, k), (v_in, v), (q_in, q), (u_in, u)))
+    ]
+    for copy in stages:
+        copy.start()
+
     barrier = pltpu.get_barrier_semaphore()
     for step in range(1, n_dp):
         pl.semaphore_signal(barrier, inc=1, device_id=((d + step) % n_dp, z), device_id_type=MESH)
@@ -266,12 +274,6 @@
             pltpu.make_async_copy(u.at[rows, :, own_cols], ub.at[rows, s], local_in.at[chunk, 3]),
         ]
 
-    own_doc = pltpu.make_async_copy(doc, docs.at[n_dp + d], doc_local)
-    own_doc.start()
-    for chunk in range(CHUNKS):
-        for copy in local_in_copies(chunk):
-            copy.start()
-
     for offset in range(1, REACH + 1):
 
         @pl.when(place < offset)
@@ -291,6 +293,10 @@
         docs[0:n_dp] = jnp.zeros((n_dp, 1, n_dp * SLAB), jnp.int32)
 
     pl.semaphore_wait(barrier, n_dp - 1 + n_dp * planes)
+
+    stages[0].wait()
+    own_doc = pltpu.make_async_copy(doc, docs.at[n_dp + d], doc_local)
+    own_doc.start()
 
     def doc_near(step):
         return remote(
@@ -354,7 +360,12 @@
             act(forward_sibling(chunk, kind))
             act(half_over(chunk, kind))
 
+    for copy in stages[1:]:
+        copy.wait()
     for chunk in range(CHUNKS):
+        for copy in local_in_copies(chunk):
+            copy.start()
+    for chunk in range(AHEAD):
         send_forward(chunk, lambda copy: copy.start())
 
     own_doc.wait()
@@ -518,6 +529,11 @@
 
     def step(chunk, carry):
         await_inputs(chunk)
+
+        @pl.when(chunk + AHEAD < CHUNKS)
+        def _():
+            send_forward(chunk + AHEAD, lambda copy: copy.start())
+
         compute(chunk)
         send_backward(chunk, lambda copy: copy.start())
         for which in range(4):
@@ -582,6 +598,15 @@
     lax.fori_loop(0, CHUNKS, drain, 0)
 
 
+def store(att, dq, dk, dv, att_out, dq_out, dk_out, dv_out, done):
+    pairs = ((att, att_out), (dq, dq_out), (dk, dk_out), (dv, dv_out))
+    copies = [pltpu.make_async_copy(src, dst, done.at[i]) for i, (src, dst) in enumerate(pairs)]
+    for copy in copies:
+        copy.start()
+    for copy in copies:
+        copy.wait()
+
+
 def direct(n_dp, n_seq, queries, keys, values, upstream, doc_ids):
     wide = (ROWS, SLAB, QUERY_HEADS * HEAD_DIMENSION)
     narrow = (ROWS, SLAB, KEY_VALUE_HEADS * HEAD_DIMENSION)
@@ -591,9 +616,14 @@
     results = pl.pallas_call(
         functools.partial(kernel, n_dp, n_seq),
         out_shape=[jax.ShapeDtypeStruct(shape, half) for shape in (wide, wide, narrow, narrow)],
-        in_specs=[anywhere] * 5,
+        in_specs=[pl.BlockSpec(memory_space=pltpu.HBM)] * 5,
         out_specs=[anywhere] * 4,
         scratch_shapes=[
+            pltpu.VMEM(wide, half),
+            pltpu.VMEM(narrow, half),
+            pltpu.VMEM(narrow, half),
+            pltpu.VMEM(wide, half),
+            pltpu.VMEM((1, n_dp * SLAB), jnp.int32),
             pltpu.VMEM((ROWS, 2, SLAB, HALF_Q), half),
             pltpu.VMEM((ROWS, 2, SLAB, HALF_Q), half),
             pltpu.VMEM((ROWS, SLOTS, SLAB, HALF_K), half),
@@ -609,6 +639,7 @@
             pltpu.VMEM((2 * n_dp, 1, n_dp * SLAB), jnp.int32),
             pltpu.VMEM((n_dp, 2 * n_dp * SLAB), jnp.int32),
             pltpu.VMEM((ROWS, WINDOW, 128), jnp.float32),
+            dma((5,)),
             dma((2 * n_dp,)),
             dma((2 * n_dp,)),
             dma(()),
@@ -629,11 +660,24 @@
         ),
         cost_estimate=pl.CostEstimate(flops=10**9, bytes_accessed=10**7, transcendentals=10**6),
     )(
-        queries.reshape(wide), keys.reshape(narrow), values.reshape(narrow),
-        upstream.reshape(wide), doc_ids,
-    )
+        *[
+            pltpu.with_memory_space_constraint(array, pltpu.HBM)
+            for array in (
+                queries.reshape(wide), keys.reshape(narrow), values.reshape(narrow),
+                upstream.reshape(wide), doc_ids,
+            )
+        ]
+    )
+    stored = pl.pallas_call(
+        store,
+        out_shape=[jax.ShapeDtypeStruct(shape, half) for shape in (wide, wide, narrow, narrow)],
+        in_specs=[anywhere] * 4,
+        out_specs=[pl.BlockSpec(memory_space=pltpu.HBM)] * 4,
+        scratch_shapes=[dma((4,))],
+        compiler_params=pltpu.CompilerParams(vmem_limit_bytes=4 * 1024 * 1024),
+    )(*results)
     tokens = ROWS * SLAB
-    return tuple(array.reshape(1, tokens, array.shape[-1]) for array in results)
+    return tuple(array.reshape(1, tokens, array.shape[-1]) for array in stored)
 
 
 def arranged(n_dp, n_seq, queries, keys, values, upstream, doc_ids):

time: 37.6 us -> 31.4 us (0.84)
  local copies, waits for them, and re-layouts: 7.44 us -> 0 us
  Pallas kernels: 29.2 us -> 30.4 us
    unnamed x14 -> x0, local copies, waits for them, and re-layouts: 7.44 us -> none
    pallas_call x0 -> x1, Pallas kernels: none -> 1.08 us  [direct(): pl.pallas_call(store, out_shape=[jax.ShapeDtypeStruct(shape, half) for sh...]
where the time goes in v2:
time: 31.4 us; the launch traced here: 31.1 us
  Pallas kernels  30.4 us (97%)
  between operations  0.64 us (2%)
    pallas_call x1, Pallas kernels, direct(): pl.pallas_call(functools.partial(kernel, n_dp, n_seq), out_shape=[jax.Sha...  29.4 us
    pallas_call x1, Pallas kernels, direct(): pl.pallas_call(store, out_shape=[jax.ShapeDtypeStruct(shape, half) for sh...  1.08 us

profile of v2, /device:TPU:0, one launch (start us, length us, event | category | flops | bytes accessed | tf_op | source)
XLA Modules:
  0.0 31.1 jit_solution(7553767192380415781)
XLA Ops:
  0.6 29.4 %shard_map.84 = (bf16[8,16,2048]{2,1,0:T(8,128)(2,1)S(1)}, bf16[8,16,2048]{2,1,0:T(8,128)(2,1)S(1)}, bf16[8,16,512]{2,1,0:T(8,128)(2,1)S(1)}, bf16[8,16,512]{2,1,0:T(8,128)(2,1)S(1)}) custom-call(bf16[8,16,2048]{2,1,0:T(8,128)(2,1)} %bitcast.8, bf16[8,16,512]{2,1,0:T(8,128)(2,1)} %bitcast.12, bf16[8,16,512]{2,1,0:T(8,128)(2,1)} %bitcast.13, ...), custom_call_target="tpu_custom_call" | custom-call | flops 1000000000 | bytes 10000000 | tf_op jit(solution)/shard_map/pallas_call | solution.py:616
  30.0 1.1 %shard_map.85 = (bf16[8,16,2048]{2,1,0:T(8,128)(2,1)}, bf16[8,16,2048]{2,1,0:T(8,128)(2,1)}, bf16[8,16,512]{2,1,0:T(8,128)(2,1)}, bf16[8,16,512]{2,1,0:T(8,128)(2,1)}) custom-call(bf16[8,16,2048]{2,1,0:T(8,128)(2,1)S(1)} %get-tuple-element.12.att, bf16[8,16,2048]{2,1,0:T(8,128)(2,1)S(1)} %get-tuple-element.13.dq, ...), custom_call_target="tpu_custom_call" | custom-call | tf_op jit(solution)/shard_map/pallas_call | solution.py:671

commit v3 on v2

--- a/solution.py
+++ b/solution.py
@@ -347,7 +347,7 @@
             half_send.at[chunk, kind], half_recv.at[chunk, kind], sibling,
         )
 
-    def send_forward(chunk, act):
+    def send_far(chunk, act):
         for offset in range(REACH, 0, -1):
 
             @pl.when(place + offset <= last)
@@ -356,17 +356,21 @@
                     for core in range(2):
                         act(forward(chunk, kind, offset, core))
 
+    def send_near(chunk, act):
         for kind in range(2):
             act(forward_sibling(chunk, kind))
             act(half_over(chunk, kind))
 
-    for copy in stages[1:]:
+    for copy in stages[1:3]:
+        copy.wait()
+    for chunk in range(AHEAD):
+        send_far(chunk, lambda copy: copy.start())
+    for copy in stages[3:]:
         copy.wait()
     for chunk in range(CHUNKS):
+        send_near(chunk, lambda copy: copy.start())
         for copy in local_in_copies(chunk):
             copy.start()
-    for chunk in range(AHEAD):
-        send_forward(chunk, lambda copy: copy.start())
 
     own_doc.wait()
     for step in range(1, n_dp):
@@ -532,7 +536,7 @@
 
         @pl.when(chunk + AHEAD < CHUNKS)
         def _():
-            send_forward(chunk + AHEAD, lambda copy: copy.start())
+            send_far(chunk + AHEAD, lambda copy: copy.start())
 
         compute(chunk)
         send_backward(chunk, lambda copy: copy.start())
@@ -583,7 +587,8 @@
 
     def drain(chunk, carry):
         rows = rows_of(chunk)
-        send_forward(chunk, lambda copy: copy.wait_send())
+        send_far(chunk, lambda copy: copy.wait_send())
+        send_near(chunk, lambda copy: copy.wait_send())
         send_backward(chunk, lambda copy: copy.wait_send())
         for kind in range(2):
             src, dst = ((ob, att), (gb, dq))[kind]

time: 31.4 us -> 31.2 us (level)
  no operation moved by 1% of the time
where the time goes in v3:
time: 31.2 us; the launch traced here: 30.9 us
  Pallas kernels  30.2 us (97%)
  between operations  0.64 us (2%)
    pallas_call x1, Pallas kernels, direct(): pl.pallas_call(functools.partial(kernel, n_dp, n_seq), out_shape=[jax.Sha...  29.1 us
    pallas_call x1, Pallas kernels, direct(): pl.pallas_call(store, out_shape=[jax.ShapeDtypeStruct(shape, half) for sh...  1.08 us

profile of v3, /device:TPU:0, one launch (start us, length us, event | category | flops | bytes accessed | tf_op | source)
XLA Modules:
  0.0 30.9 jit_solution(15055737349419553020)
XLA Ops:
  0.6 29.1 %shard_map.84 = (bf16[8,16,2048]{2,1,0:T(8,128)(2,1)S(1)}, bf16[8,16,2048]{2,1,0:T(8,128)(2,1)S(1)}, bf16[8,16,512]{2,1,0:T(8,128)(2,1)S(1)}, bf16[8,16,512]{2,1,0:T(8,128)(2,1)S(1)}) custom-call(bf16[8,16,2048]{2,1,0:T(8,128)(2,1)} %bitcast.8, bf16[8,16,512]{2,1,0:T(8,128)(2,1)} %bitcast.12, bf16[8,16,512]{2,1,0:T(8,128)(2,1)} %bitcast.13, ...), custom_call_target="tpu_custom_call" | custom-call | flops 1000000000 | bytes 10000000 | tf_op jit(solution)/shard_map/pallas_call | solution.py:621
  29.8 1.1 %shard_map.85 = (bf16[8,16,2048]{2,1,0:T(8,128)(2,1)}, bf16[8,16,2048]{2,1,0:T(8,128)(2,1)}, bf16[8,16,512]{2,1,0:T(8,128)(2,1)}, bf16[8,16,512]{2,1,0:T(8,128)(2,1)}) custom-call(bf16[8,16,2048]{2,1,0:T(8,128)(2,1)S(1)} %get-tuple-element.12.att, bf16[8,16,2048]{2,1,0:T(8,128)(2,1)S(1)} %get-tuple-element.13.dq, ...), custom_call_target="tpu_custom_call" | custom-call | tf_op jit(solution)/shard_map/pallas_call | solution.py:676
